TPU v7x, 512 devices: a whole 4x4x16 slice. The times are simulated.
512 devices in a mesh: dp: 8 (over x, core), expouter: 8 (over z_lo), expinner: 8 (over z_hi, y).
Axes of the slice: x: 4, y: 4, z: 16 (z_hi: 2, z_lo: 8; z = z_hi * 8 + z_lo), core: 2. Of those that a mesh axis runs over, the one named last changes fastest.
Arguments:
- tokens: bfloat16 [65536, 1024], P(('dp', 'expouter', 'expinner')), may hold values from -6 to 6
- cotangent: bfloat16 [65536, 1024], P(('dp', 'expouter', 'expinner')), may hold values from -6 to 6
- gate_probs: float32 [65536, 2], P(('dp', 'expouter', 'expinner')), may hold values from 0.05 to 1
- expert_ids: int32 [65536, 2], P(('dp', 'expouter', 'expinner')), may hold values from 0 to 63, all different within a row; in each aligned block of 128 rows (0 to 127, 128 to 255, ...) at most 5 rows name the same one
- gate_weight: bfloat16 [64, 1024, 768], P(('expouter', 'expinner'), 'dp'), may hold values from -0.1875 to 0.1875
- up_weight: bfloat16 [64, 1024, 768], P(('expouter', 'expinner'), 'dp'), may hold values from -0.1875 to 0.1875
- down_weight: bfloat16 [64, 1024, 768], P(('expouter', 'expinner'), 'dp'), may hold values from -0.21875 to 0.21875
Outputs:
- mixed: bfloat16 [65536, 1024], P(('dp', 'expouter', 'expinner'))
- grad_tokens: bfloat16 [65536, 1024], P(('dp', 'expouter', 'expinner'))
- grad_probs: float32 [65536, 2], P(('dp', 'expouter', 'expinner'))
- grad_gate: float32 [64, 1024, 768], P(('expouter', 'expinner'), 'dp')
- grad_up: float32 [64, 1024, 768], P(('expouter', 'expinner'), 'dp')
- grad_down: float32 [64, 1024, 768], P(('expouter', 'expinner'), 'dp')
Inputs may be any that keep to these rules, and one draw needn't show every extreme that they name: `expert_ids`: among the tokens of one device (aligned blocks of 128 tokens) no expert is named more than 5 times, a bound that some block reaches; a token's 2 experts differ.
All inputs are finite; a program needn't handle non-finite values.
Results may differ from a plain program's by a relative error of at most 0.0065.
Values may be sent and summed in bfloat16 or wider, within the bound.
A program may use at most 64 MiB of HBM per device.

v0:
```python
import jax
import jax.numpy as jnp
from jax import lax
from jax.sharding import PartitionSpec as P


def expert_pass(rows_x, rows_o, gate_mat, up_mat, down_mat):
    pre_gate = jnp.dot(rows_x, gate_mat, preferred_element_type=jnp.float32)
    pre_up = jnp.dot(rows_x, up_mat, preferred_element_type=jnp.float32)
    sigma = jax.nn.sigmoid(pre_gate)
    active = pre_gate * sigma
    hidden = (active * pre_up).astype(jnp.bfloat16)
    expert_out = jnp.dot(hidden, down_mat.T, preferred_element_type=jnp.float32).astype(
        jnp.bfloat16
    )
    grad_hidden = jnp.dot(rows_o, down_mat, preferred_element_type=jnp.float32)
    slope = sigma * (1.0 + pre_gate * (1.0 - sigma))
    grad_gate_pre = (grad_hidden * pre_up * slope).astype(jnp.bfloat16)
    grad_up_pre = (grad_hidden * active).astype(jnp.bfloat16)
    grad_rows = (
        jnp.dot(grad_gate_pre, gate_mat.T, preferred_element_type=jnp.float32)
        + jnp.dot(grad_up_pre, up_mat.T, preferred_element_type=jnp.float32)
    ).astype(jnp.bfloat16)
    return (hidden, expert_out, grad_gate_pre, grad_up_pre, grad_rows)


def contract_rows(left, right):
    return lax.dot_general(
        left, right, (((0,), (0,)), ((), ())), preferred_element_type=jnp.float32
    )


def per_device(tokens, cotangent, gate_probs, expert_ids, gate_weight, up_weight, down_weight):
    tok_rows, model_width = tokens.shape
    top_count = expert_ids.shape[1]
    outer_count = lax.axis_size("expouter")
    inner_count = lax.axis_size("expinner")
    expert_count = outer_count * inner_count
    capacity = max(2, tok_rows * top_count * 5 // (4 * expert_count))
    slots_all = expert_count * capacity
    assigns = tok_rows * top_count
    flat_route = expert_ids.reshape(assigns)
    onehot = (flat_route[:, None] == jnp.arange(expert_count, dtype=jnp.int32)[None, :]).astype(
        jnp.int32
    )
    earlier = jnp.cumsum(onehot, axis=0) - onehot
    slot_pos = jnp.sum(earlier * onehot, axis=1)
    target = flat_route * capacity + slot_pos
    select = (target[None, :] == jnp.arange(slots_all, dtype=jnp.int32)[:, None]).astype(
        jnp.bfloat16
    )
    token_select = select.reshape(slots_all, tok_rows, top_count).sum(axis=2)
    send_x = jnp.dot(token_select, tokens, preferred_element_type=jnp.float32).astype(jnp.bfloat16)
    scaled = (gate_probs[:, :, None] * cotangent[:, None, :].astype(jnp.float32)).astype(
        jnp.bfloat16
    )
    send_o = jnp.dot(
        select, scaled.reshape(assigns, model_width), preferred_element_type=jnp.float32
    ).astype(jnp.bfloat16)
    weights_all = (
        lax.all_gather(gate_weight, "dp", axis=1, tiled=True),
        lax.all_gather(up_weight, "dp", axis=1, tiled=True),
        lax.all_gather(down_weight, "dp", axis=1, tiled=True),
    )
    gate_full = weights_all[0][0]
    up_full = weights_all[1][0]
    down_full = weights_all[2][0]
    shaped = (
        send_x.reshape(expert_count, capacity, model_width),
        send_o.reshape(expert_count, capacity, model_width),
    )
    recv_x, recv_o = (
        lax.all_to_all(
            shaped[0], ("expouter", "expinner"), split_axis=0, concat_axis=0, tiled=True
        ),
        lax.all_to_all(
            shaped[1], ("expouter", "expinner"), split_axis=0, concat_axis=0, tiled=True
        ),
    )
    rows_x = recv_x.reshape(slots_all, model_width)
    rows_o = recv_o.reshape(slots_all, model_width)
    hidden, expert_out, grad_gate_pre, grad_up_pre, grad_rows = expert_pass(
        rows_x, rows_o, gate_full, up_full, down_full
    )
    returned = (
        expert_out.reshape(expert_count, capacity, model_width),
        grad_rows.reshape(expert_count, capacity, model_width),
    )
    back_out, back_grad = (
        lax.all_to_all(
            returned[0], ("expouter", "expinner"), split_axis=0, concat_axis=0, tiled=True
        ),
        lax.all_to_all(
            returned[1], ("expouter", "expinner"), split_axis=0, concat_axis=0, tiled=True
        ),
    )
    pick_out = back_out.reshape(slots_all, model_width)[target].reshape(
        tok_rows, top_count, model_width
    )
    pick_grad = back_grad.reshape(slots_all, model_width)[target].reshape(
        tok_rows, top_count, model_width
    )
    pick_float = pick_out.astype(jnp.float32)
    mixed = jnp.sum(gate_probs[:, :, None] * pick_float, axis=1).astype(jnp.bfloat16)
    grad_tokens = jnp.sum(pick_grad.astype(jnp.float32), axis=1).astype(jnp.bfloat16)
    grad_probs = jnp.sum(cotangent[:, None, :].astype(jnp.float32) * pick_float, axis=2)
    cols_x, cols_o = (
        lax.all_to_all(rows_x, "dp", split_axis=1, concat_axis=0, tiled=True),
        lax.all_to_all(rows_o, "dp", split_axis=1, concat_axis=0, tiled=True),
    )
    grad_g = contract_rows(cols_x, lax.all_gather(grad_gate_pre, "dp", axis=0, tiled=True))
    grad_u = contract_rows(cols_x, lax.all_gather(grad_up_pre, "dp", axis=0, tiled=True))
    grad_d = contract_rows(cols_o, lax.all_gather(hidden, "dp", axis=0, tiled=True))
    return (mixed, grad_tokens, grad_probs, grad_g[None], grad_u[None], grad_d[None])


def solution(mesh):
    return jax.shard_map(
        per_device,
        mesh=mesh,
        in_specs=(
            P(("dp", "expouter", "expinner"), None),
            P(("dp", "expouter", "expinner"), None),
            P(("dp", "expouter", "expinner"), None),
            P(("dp", "expouter", "expinner"), None),
            P(("expouter", "expinner"), "dp", None),
            P(("expouter", "expinner"), "dp", None),
            P(("expouter", "expinner"), "dp", None),
        ),
        out_specs=(
            P(("dp", "expouter", "expinner"), None),
            P(("dp", "expouter", "expinner"), None),
            P(("dp", "expouter", "expinner"), None),
            P(("expouter", "expinner"), "dp", None),
            P(("expouter", "expinner"), "dp", None),
            P(("expouter", "expinner"), "dp", None),
        ),
        check_vma=False,
    )
```

profile of v0, /device:TPU:1, one launch (start us, length us, event | category | flops | bytes accessed | tf_op | source)
XLA Modules:
  0.0 330.3 jit_solution(10053245813468858572)
XLA Ops:
  7.2 0.7 all-gather.9.cloned.1.call-update
  7.9 0.8 copy.33
  9.0 0.6 reduce-window.6
  10.3 0.3 convolution_convert_fusion
  10.6 1.2 reshape.131
  11.8 19.4 %all-to-all-start = ((bf16[64,5,1024]{2,1,0:T(8,128)(2,1)}), bf16[64,5,1024]{2,1,0:T(8,128)(2,1)S(1)}, u32[]{:S(2)}, u32[]{:S(2)}) async-start(bf16[64,5,1024]{2,1,0:T(8,128)(2,1)} %reshape.131), calls=%async_computation | async-start | bytes 2097152 | tf_op jit(solution)/shard_map/all_to_all | solution.py:73
  31.3 0.7 all-gather.11.cloned.1.call-update
  32.3 0.3 mul.97
  32.6 0.7 mul.98
  33.3 0.4 convolution_convert_fusion.1
  33.7 1.2 reshape.135
  35.0 48.6 %all-to-all-done = bf16[64,5,1024]{2,1,0:T(8,128)(2,1)S(1)} async-done(((bf16[64,5,1024]{2,1,0:T(8,128)(2,1)}), bf16[64,5,1024]{2,1,0:T(8,128)(2,1)S(1)}, u32[]{:S(2)}, u32[]{:S(2)}) %all-to-all-start) | async-done | bytes 655392 | tf_op jit(solution)/shard_map/all_to_all | solution.py:73
  83.6 8.3 %all-to-all-start.2 = ((bf16[64,5,1024]{2,1,0:T(8,128)(2,1)}), bf16[64,5,1024]{2,1,0:T(8,128)(2,1)S(1)}, u32[]{:S(2)}, u32[]{:S(2)}) async-start(bf16[64,5,1024]{2,1,0:T(8,128)(2,1)} %reshape.135), calls=%async_computation.2 | async-start | bytes 2097152 | tf_op jit(solution)/shard_map/all_to_all | solution.py:76
  91.9 0.7 all-gather.7.cloned.1.call-update
  92.9 51.8 %all-to-all-done.2 = bf16[64,5,1024]{2,1,0:T(8,128)(2,1)S(1)} async-done(((bf16[64,5,1024]{2,1,0:T(8,128)(2,1)}), bf16[64,5,1024]{2,1,0:T(8,128)(2,1)S(1)}, u32[]{:S(2)}, u32[]{:S(2)}) %all-to-all-start.2) | async-done | bytes 655392 | tf_op jit(solution)/shard_map/all_to_all | solution.py:76
  144.7 1.1 reshape.136
  145.8 3.1 fusion.6
  148.9 3.2 fusion
  152.2 4.1 %multiply_convert_fusion.2 = (bf16[320,768]{1,0:T(8,128)(2,1)}, bf16[320,768]{1,0:T(8,128)(2,1)}, bf16[320,768]{1,0:T(8,128)(2,1)}) fusion(f32[320,768]{1,0:T(8,128)} %fusion, f32[320,768]{1,0:T(8,128)} %fusion.6, bf16[320,1024]{1,0:T(8,128)(2,1)S(1)} %reshape.132, bf16[1,1024,768]{2,1,0:T(8,128)(2,1)} %all-gather.7.cloned.1.call-done), kind=kOutput, calls=%fused_computation.26 | convolution fusion | flops 507002880 | bytes 5668864 | tf_op jit(solution)/shard_map/dot_general | solution.py:8
  156.3 0.5 all-gather.15.cloned.1.call-update
  156.9 0.5 all-gather.17.cloned.1.call-update
  157.5 2.3 fusion.4
  159.7 0.7 fusion.18
  160.5 1.2 reshape.137
  161.7 7.4 %all-to-all-start.3 = ((bf16[64,5,1024]{2,1,0:T(8,128)(2,1)}), bf16[64,5,1024]{2,1,0:T(8,128)(2,1)S(1)}, u32[]{:S(2)}, u32[]{:S(2)}) async-start(bf16[64,5,1024]{2,1,0:T(8,128)(2,1)} %reshape.137), calls=%async_computation.3 | async-start | bytes 2097152 | tf_op jit(solution)/shard_map/all_to_all | solution.py:93
  169.0 3.2 fusion.15
  172.2 2.2 reshape.133
  174.4 47.6 %all-to-all-done.3 = bf16[64,5,1024]{2,1,0:T(8,128)(2,1)S(1)} async-done(((bf16[64,5,1024]{2,1,0:T(8,128)(2,1)}), bf16[64,5,1024]{2,1,0:T(8,128)(2,1)S(1)}, u32[]{:S(2)}, u32[]{:S(2)}) %all-to-all-start.3) | async-done | bytes 655392 | tf_op jit(solution)/shard_map/all_to_all | solution.py:93
  222.0 7.4 %all-to-all-start.1 = ((bf16[64,5,1024]{2,1,0:T(8,128)(2,1)}), bf16[64,5,1024]{2,1,0:T(8,128)(2,1)}, u32[]{:S(2)}, u32[]{:S(2)}) async-start(bf16[64,5,1024]{2,1,0:T(8,128)(2,1)} %reshape.133), calls=%async_computation.1 | async-start | bytes 2097152 | tf_op jit(solution)/shard_map/all_to_all | solution.py:90
  229.4 1.8 convert_element_type.67
  231.4 1.6 all_to_all.44
  233.0 2.0 copy.39
  235.0 46.0 %all-to-all-done.1 = bf16[64,5,1024]{2,1,0:T(8,128)(2,1)} async-done(((bf16[64,5,1024]{2,1,0:T(8,128)(2,1)}), bf16[64,5,1024]{2,1,0:T(8,128)(2,1)}, u32[]{:S(2)}, u32[]{:S(2)}) %all-to-all-start.1) | async-done | bytes 655392 | tf_op jit(solution)/shard_map/all_to_all | solution.py:90
  280.9 8.3 %all-to-all-start.4 = ((bf16[320,8,128]{2,0,1:T(8,128)(2,1)}), bf16[320,8,128]{2,0,1:T(8,128)(2,1)S(1)}, u32[]{:S(2)}, u32[]{:S(2)}) async-start(bf16[320,8,128]{2,0,1:T(8,128)(2,1)} %copy.39), calls=%async_computation.4 | async-start | bytes 1310720 | tf_op jit(solution)/shard_map/all_to_all | solution.py:108
  289.2 1.6 all_to_all.48
  290.8 2.1 copy.40
  293.2 1.2 gather_fusion.1
  294.5 1.4 reshape.134
  296.0 1.2 gather_fusion
  297.1 0.7 reshape.140
  297.8 3.6 %multiply_reduce_fusion = (f32[128,2]{1,0:T(8,128)S(1)}, bf16[128,1024]{1,0:T(8,128)(2,1)}) fusion(f32[128,2,1024]{2,1,0:T(2,128)S(1)} %reshape.140, f32[128,1024]{1,0:T(8,128)} %convert_element_type.67, f32[128,2]{1,0:T(8,128)S(1)} %copy.32), kind=kLoop, calls=%fused_computation.22 | loop fusion | flops 917248 | bytes 1837056 | tf_op jit(solution)/shard_map/reduce_sum | solution.py:106
  301.4 0.6 copy.41
  302.0 2.1 reduce_sum.60
  304.1 4.8 %all-to-all-start.5 = ((bf16[320,8,128]{2,0,1:T(8,128)(2,1)}), bf16[320,8,128]{2,0,1:T(8,128)(2,1)S(1)}, u32[]{:S(2)}, u32[]{:S(2)}) async-start(bf16[320,8,128]{2,0,1:T(8,128)(2,1)} %copy.40), calls=%async_computation.5 | async-start | bytes 1310720 | tf_op jit(solution)/shard_map/all_to_all | solution.py:109
  308.9 3.6 %convolution_bitcast_fusion.2 = f32[1,128,768]{2,1,0:T(8,128)} fusion(bf16[2560,128]{1,0:T(8,128)(2,1)S(1)} %bitcast.70, bf16[2560,768]{1,0:T(8,128)(2,1)} %all-gather.13.cloned.1.call-done), kind=kOutput, calls=%fused_computation.21 | convolution fusion | flops 503316480 | bytes 4980736 | tf_op jit(solution)/shard_map/dot_general | solution.py:28
  312.5 3.6 %convolution_bitcast_fusion.1 = f32[1,128,768]{2,1,0:T(8,128)} fusion(bf16[2560,128]{1,0:T(8,128)(2,1)S(1)} %bitcast.71, bf16[2560,768]{1,0:T(8,128)(2,1)} %all-gather.15.cloned.1.call-done), kind=kOutput, calls=%fused_computation.20 | convolution fusion | flops 503316480 | bytes 4980736 | tf_op jit(solution)/shard_map/dot_general | solution.py:28
  316.1 3.7 %all-to-all-done.5 = bf16[320,8,128]{2,0,1:T(8,128)(2,1)S(1)} async-done(((bf16[320,8,128]{2,0,1:T(8,128)(2,1)}), bf16[320,8,128]{2,0,1:T(8,128)(2,1)S(1)}, u32[]{:S(2)}, u32[]{:S(2)}) %all-to-all-start.5) | async-done | bytes 655392 | tf_op jit(solution)/shard_map/all_to_all | solution.py:109
  319.8 3.6 %convolution_bitcast_fusion = f32[1,128,768]{2,1,0:T(8,128)} fusion(bf16[2560,128]{1,0:T(8,128)(2,1)S(1)} %bitcast.72, bf16[2560,768]{1,0:T(8,128)(2,1)} %all-gather.17.cloned.1.call-done), kind=kOutput, calls=%fused_computation.19 | convolution fusion | flops 503316480 | bytes 4980736 | tf_op jit(solution)/shard_map/dot_general | solution.py:28
  (46 shorter events, 2.3 us)
Async XLA Ops:
  7.2 3.1 copy-start
  7.2 138.7 %all-gather.9.cloned.1.call-start = ((), (), s32[]{:S(2)}) async-start(), calls=%async_computation.7 | async-start | bytes 1769472 | tf_op jit(solution)/shard_map/all_gather | solution.py:62
  11.8 20.2 %copy-start.5 = (f32[128,2]{0,1:T(2,128)S(1)}, f32[128,2]{0,1:T(2,128)}, u32[]{:S(2)}) copy-start(f32[128,2]{0,1:T(2,128)} %param.9) | copy-start | bytes 3076
  11.8 20.4 %copy-start.4 = (bf16[128,1024]{1,0:T(8,128)(2,1)S(1)}, bf16[128,1024]{1,0:T(8,128)(2,1)}, u32[]{:S(2)}) copy-start(bf16[128,1024]{1,0:T(8,128)(2,1)} %param.8) | copy-start | bytes 786436
  11.8 71.7 %all-to-all-start = ((bf16[64,5,1024]{2,1,0:T(8,128)(2,1)}), bf16[64,5,1024]{2,1,0:T(8,128)(2,1)S(1)}, u32[]{:S(2)}, u32[]{:S(2)}) async-start(bf16[64,5,1024]{2,1,0:T(8,128)(2,1)} %reshape.131), calls=%async_computation | async-start | bytes 2097152 | tf_op jit(solution)/shard_map/all_to_all | solution.py:73
  31.3 117.7 %all-gather.11.cloned.1.call-start = ((), (), s32[]{:S(2)}) async-start(), calls=%async_computation.8 | async-start | bytes 1769472 | tf_op jit(solution)/shard_map/all_gather | solution.py:63
  83.6 61.1 %all-to-all-start.2 = ((bf16[64,5,1024]{2,1,0:T(8,128)(2,1)}), bf16[64,5,1024]{2,1,0:T(8,128)(2,1)S(1)}, u32[]{:S(2)}, u32[]{:S(2)}) async-start(bf16[64,5,1024]{2,1,0:T(8,128)(2,1)} %reshape.135), calls=%async_computation.2 | async-start | bytes 2097152 | tf_op jit(solution)/shard_map/all_to_all | solution.py:76
  91.9 60.3 %all-gather.7.cloned.1.call-start = ((), (), s32[]{:S(2)}) async-start(), calls=%async_computation.6 | async-start | bytes 1769472 | tf_op jit(solution)/shard_map/all_gather | solution.py:61
  92.6 216.3 %all-gather.13.cloned.1.call-start = ((), (), s32[]{:S(2)}) async-start(), calls=%async_computation.9 | async-start | bytes 4423680 | tf_op jit(solution)/shard_map/all_gather | solution.py:111
  156.2 1.2 copy-start.1
  156.3 156.3 %all-gather.15.cloned.1.call-start = ((), (), s32[]{:S(2)}) async-start(), calls=%async_computation.10 | async-start | bytes 4423680 | tf_op jit(solution)/shard_map/all_gather | solution.py:112
  156.9 163.0 %all-gather.17.cloned.1.call-start = ((), (), s32[]{:S(2)}) async-start(), calls=%async_computation.11 | async-start | bytes 4423680 | tf_op jit(solution)/shard_map/all_gather | solution.py:113
  157.4 2.3 copy-start.2
  157.4 2.3 copy-start.3
  161.7 60.3 %all-to-all-start.3 = ((bf16[64,5,1024]{2,1,0:T(8,128)(2,1)}), bf16[64,5,1024]{2,1,0:T(8,128)(2,1)S(1)}, u32[]{:S(2)}, u32[]{:S(2)}) async-start(bf16[64,5,1024]{2,1,0:T(8,128)(2,1)} %reshape.137), calls=%async_computation.3 | async-start | bytes 2097152 | tf_op jit(solution)/shard_map/all_to_all | solution.py:93
  222.0 59.0 %all-to-all-start.1 = ((bf16[64,5,1024]{2,1,0:T(8,128)(2,1)}), bf16[64,5,1024]{2,1,0:T(8,128)(2,1)}, u32[]{:S(2)}, u32[]{:S(2)}) async-start(bf16[64,5,1024]{2,1,0:T(8,128)(2,1)} %reshape.133), calls=%async_computation.1 | async-start | bytes 2097152 | tf_op jit(solution)/shard_map/all_to_all | solution.py:90
  280.9 23.2 %all-to-all-start.4 = ((bf16[320,8,128]{2,0,1:T(8,128)(2,1)}), bf16[320,8,128]{2,0,1:T(8,128)(2,1)S(1)}, u32[]{:S(2)}, u32[]{:S(2)}) async-start(bf16[320,8,128]{2,0,1:T(8,128)(2,1)} %copy.39), calls=%async_computation.4 | async-start | bytes 1310720 | tf_op jit(solution)/shard_map/all_to_all | solution.py:108
  304.1 15.7 %all-to-all-start.5 = ((bf16[320,8,128]{2,0,1:T(8,128)(2,1)}), bf16[320,8,128]{2,0,1:T(8,128)(2,1)S(1)}, u32[]{:S(2)}, u32[]{:S(2)}) async-start(bf16[320,8,128]{2,0,1:T(8,128)(2,1)} %copy.40), calls=%async_computation.5 | async-start | bytes 1310720 | tf_op jit(solution)/shard_map/all_to_all | solution.py:109
Sparse Core Ops, SparseCore 0:
  10.1 37.8 all-gather.8
  50.2 32.1 all-gather.10
  94.8 34.0 all-gather.6
  156.4 33.3 all-gather.12
  191.8 38.6 all-gather.14
  232.5 38.6 all-gather.16
where the time goes:
time: 331 us; the launch traced here: 330 us
  waiting for transfers between devices  201 us (61%)
  starting transfers between devices  55.8 us (17%)
  matrix products  28 us (8%)
  local copies, waits for them, and re-layouts  22.9 us (7%)
  between operations  14.4 us (4%)
  other arithmetic  8.38 us (3%)
    all_to_all x1, waiting for transfers between devices, per_device(): lax.all_to_all(shaped[1], ('expouter', 'expinner'), split_axis=0, concat_...  51.8 us
    all_to_all x1, waiting for transfers between devices, per_device(): lax.all_to_all(shaped[0], ('expouter', 'expinner'), split_axis=0, concat_...  48.6 us
    all_to_all x1, waiting for transfers between devices, per_device(): lax.all_to_all(returned[1], ('expouter', 'expinner'), split_axis=0, conca...  47.6 us
    all_to_all x1, waiting for transfers between devices, per_device(): lax.all_to_all(returned[0], ('expouter', 'expinner'), split_axis=0, conca...  46 us
    all_to_all x1, starting transfers between devices, per_device(): lax.all_to_all(shaped[0], ('expouter', 'expinner'), split_axis=0, concat_...  19.4 us
    dot_general x3, matrix products, contract_rows(): lax.dot_general(left, right, (((0,), (0,)), ((), ())), preferred_element_...  10.8 us
    all_to_all x1, starting transfers between devices, per_device(): lax.all_to_all(shaped[1], ('expouter', 'expinner'), split_axis=0, concat_...  8.28 us
    all_to_all x1, starting transfers between devices, per_device(): lax.all_to_all(rows_x, 'dp', split_axis=1, concat_axis=0, tiled=True)  8.27 us
  transfers between devices with their start and end apart: 12, of which 5 were waited for; matrix products, arithmetic and copies ran while one was open for 15% of the time, Pallas kernels for 0%

commit v1 on v0

--- a/solution.py
+++ b/solution.py
@@ -2,6 +2,28 @@
 import jax.numpy as jnp
 from jax import lax
 from jax.sharding import PartitionSpec as P
+
+
+def cut_along(x, dim, devices):
+    before, after = (x.shape[:dim], x.shape[dim + 1 :])
+    return jnp.moveaxis(x.reshape(*before, devices, -1, *after), dim, 0)
+
+
+def joined_along(blocks, dim):
+    blocks = jnp.moveaxis(blocks, 0, dim)
+    dims = blocks.shape
+    return blocks.reshape(*dims[:dim], dims[dim] * dims[dim + 1], *dims[dim + 2 :])
+
+
+def pairwise_exchange(x, axis, split_dim, concat_dim):
+    devices, index = (lax.axis_size(axis), lax.axis_index(axis))
+    blocks = cut_along(x, split_dim, devices)
+    outs = [blocks[index]]
+    for step in range(1, devices):
+        sent = blocks[index ^ step]
+        outs.append(lax.ppermute(sent, axis, [(i, i ^ step) for i in range(devices)]))
+    blocks = jnp.stack(outs)[index ^ jnp.arange(devices)]
+    return joined_along(blocks, concat_dim)
 
 
 def expert_pass(rows_x, rows_o, gate_mat, up_mat, down_mat):
@@ -106,7 +128,7 @@
     grad_probs = jnp.sum(cotangent[:, None, :].astype(jnp.float32) * pick_float, axis=2)
     cols_x, cols_o = (
         lax.all_to_all(rows_x, "dp", split_axis=1, concat_axis=0, tiled=True),
-        lax.all_to_all(rows_o, "dp", split_axis=1, concat_axis=0, tiled=True),
+        pairwise_exchange(rows_o, "dp", 1, 0),
     )
     grad_g = contract_rows(cols_x, lax.all_gather(grad_gate_pre, "dp", axis=0, tiled=True))
     grad_u = contract_rows(cols_x, lax.all_gather(grad_up_pre, "dp", axis=0, tiled=True))

time: 331 us -> 321 us (0.970)
  waiting for transfers between devices: 201 us -> 168 us
  starting transfers between devices: 55.8 us -> 74.4 us
  local copies, waits for them, and re-layouts: 22.9 us -> 26.3 us
    all_to_all x1, waiting for transfers between devices: 46 us -> 17.5 us  [per_device(): lax.all_to_all(returned[0], ('expouter', 'expinner'), split_axis=0, conca...]
    ppermute x0 -> x7, starting transfers between devices: none -> 23.4 us  [pairwise_exchange(): lax.ppermute(sent, axis, [(i, i ^ step) for i in range(devices)])]
    all_to_all x1 -> x0, starting transfers between devices: 4.8 us -> none  [per_device(): lax.all_to_all(rows_o, 'dp', split_axis=1, concat_axis=0, tiled=True)]
    unnamed x15 -> x39, local copies, waits for them, and re-layouts: 1.56 us -> 6.14 us
    all_to_all x1 -> x0, waiting for transfers between devices: 3.71 us -> none  [per_device(): lax.all_to_all(rows_o, 'dp', split_axis=1, concat_axis=0, tiled=True)]
    all_to_all x2 -> x0, local copies, waits for them, and re-layouts: 3.66 us -> none  [per_device(): lax.all_to_all(rows_o, 'dp', split_axis=1, concat_axis=0, tiled=True)]
  transfers between devices with their start and end apart: 12 -> 18, of which waited for: 5 -> 4; matrix products, arithmetic and copies ran while one was open for 15% -> 17% of each run, Pallas kernels for 0% -> 0%
where the time goes in v1:
time: 321 us; the launch traced here: 320 us
  waiting for transfers between devices  168 us (52%)
  starting transfers between devices  74.4 us (23%)
  matrix products  28 us (9%)
  local copies, waits for them, and re-layouts  26.3 us (8%)
  between operations  14.7 us (5%)
  other arithmetic  8.4 us (3%)
    all_to_all x1, waiting for transfers between devices, per_device(): lax.all_to_all(shaped[1], ('expouter', 'expinner'), split_axis=0, concat_...  51.8 us
    all_to_all x1, waiting for transfers between devices, per_device(): lax.all_to_all(shaped[0], ('expouter', 'expinner'), split_axis=0, concat_...  48.1 us
    all_to_all x1, waiting for transfers between devices, per_device(): lax.all_to_all(returned[1], ('expouter', 'expinner'), split_axis=0, conca...  47.6 us
    ppermute x7, starting transfers between devices, pairwise_exchange(): lax.ppermute(sent, axis, [(i, i ^ step) for i in range(devices)])  23.4 us
    all_to_all x1, starting transfers between devices, per_device(): lax.all_to_all(shaped[0], ('expouter', 'expinner'), split_axis=0, concat_...  19.4 us
    all_to_all x1, waiting for transfers between devices, per_device(): lax.all_to_all(returned[0], ('expouter', 'expinner'), split_axis=0, conca...  17.5 us
    dot_general x3, matrix products, contract_rows(): lax.dot_general(left, right, (((0,), (0,)), ((), ())), preferred_element_...  10.8 us
    all_to_all x1, starting transfers between devices, per_device(): lax.all_to_all(shaped[1], ('expouter', 'expinner'), split_axis=0, concat_...  8.32 us
  transfers between devices with their start and end apart: 18, of which 4 were waited for; matrix products, arithmetic and copies ran while one was open for 17% of the time, Pallas kernels for 0%

profile of v1, /device:TPU:1, one launch (start us, length us, event | category | flops | bytes accessed | tf_op | source)
XLA Modules:
  0.0 319.8 jit_solution(6324986407642720470)
XLA Ops:
  7.2 0.7 all-gather.9.cloned.1.call-update
  7.9 0.8 copy.31
  10.6 1.2 reshape.161
  11.8 19.4 %all-to-all-start = ((bf16[64,5,1024]{2,1,0:T(8,128)(2,1)}), bf16[64,5,1024]{2,1,0:T(8,128)(2,1)S(1)}, u32[]{:S(2)}, u32[]{:S(2)}) async-start(bf16[64,5,1024]{2,1,0:T(8,128)(2,1)} %reshape.161), calls=%async_computation | async-start | bytes 2097152 | tf_op jit(solution)/shard_map/all_to_all | solution.py:95
  31.3 0.7 all-gather.11.cloned.1.call-update
  33.0 0.7 mul.98
  34.2 1.3 reshape.165
  35.5 48.1 %all-to-all-done = bf16[64,5,1024]{2,1,0:T(8,128)(2,1)S(1)} async-done(((bf16[64,5,1024]{2,1,0:T(8,128)(2,1)}), bf16[64,5,1024]{2,1,0:T(8,128)(2,1)S(1)}, u32[]{:S(2)}, u32[]{:S(2)}) %all-to-all-start) | async-done | bytes 655392 | tf_op jit(solution)/shard_map/all_to_all | solution.py:95
  83.5 8.3 %all-to-all-start.2 = ((bf16[64,5,1024]{2,1,0:T(8,128)(2,1)}), bf16[64,5,1024]{2,1,0:T(8,128)(2,1)S(1)}, u32[]{:S(2)}, u32[]{:S(2)}) async-start(bf16[64,5,1024]{2,1,0:T(8,128)(2,1)} %reshape.165), calls=%async_computation.2 | async-start | bytes 2097152 | tf_op jit(solution)/shard_map/all_to_all | solution.py:98
  91.9 0.7 all-gather.7.cloned.1.call-update
  92.9 51.8 %all-to-all-done.2 = bf16[64,5,1024]{2,1,0:T(8,128)(2,1)S(1)} async-done(((bf16[64,5,1024]{2,1,0:T(8,128)(2,1)}), bf16[64,5,1024]{2,1,0:T(8,128)(2,1)S(1)}, u32[]{:S(2)}, u32[]{:S(2)}) %all-to-all-start.2) | async-done | bytes 655392 | tf_op jit(solution)/shard_map/all_to_all | solution.py:98
  144.7 1.1 reshape.166
  145.8 3.0 fusion.6
  148.9 3.3 %fusion = f32[320,768]{1,0:T(8,128)} fusion(bf16[320,1024]{1,0:T(8,128)(2,1)} %reshape.166, bf16[1,1024,768]{2,1,0:T(8,128)(2,1)} %all-gather.11.cloned.1.call-done), kind=kOutput, calls=%fused_computation.3 | convolution fusion | flops 503316480 | bytes 3211264 | tf_op jit(solution)/shard_map/dot_general | solution.py:38
  152.1 4.1 %multiply_convert_fusion.2 = (bf16[320,768]{1,0:T(8,128)(2,1)}, bf16[320,768]{1,0:T(8,128)(2,1)}, bf16[320,768]{1,0:T(8,128)(2,1)}) fusion(f32[320,768]{1,0:T(8,128)} %fusion, f32[320,768]{1,0:T(8,128)} %fusion.6, bf16[320,1024]{1,0:T(8,128)(2,1)S(1)} %reshape.162, bf16[1,1024,768]{2,1,0:T(8,128)(2,1)} %all-gather.7.cloned.1.call-done), kind=kOutput, calls=%fused_computation.27 | convolution fusion | flops 507002880 | bytes 5668864 | tf_op jit(solution)/shard_map/dot_general | solution.py:30
  157.4 2.3 fusion.4
  159.7 0.7 fusion.18
  160.4 1.2 reshape.167
  161.6 7.4 %all-to-all-start.3 = ((bf16[64,5,1024]{2,1,0:T(8,128)(2,1)}), bf16[64,5,1024]{2,1,0:T(8,128)(2,1)S(1)}, u32[]{:S(2)}, u32[]{:S(2)}) async-start(bf16[64,5,1024]{2,1,0:T(8,128)(2,1)} %reshape.167), calls=%async_computation.3 | async-start | bytes 2097152 | tf_op jit(solution)/shard_map/all_to_all | solution.py:115
  169.0 3.2 fusion.15
  172.2 2.2 reshape.163
  174.3 47.6 %all-to-all-done.3 = bf16[64,5,1024]{2,1,0:T(8,128)(2,1)S(1)} async-done(((bf16[64,5,1024]{2,1,0:T(8,128)(2,1)}), bf16[64,5,1024]{2,1,0:T(8,128)(2,1)S(1)}, u32[]{:S(2)}, u32[]{:S(2)}) %all-to-all-start.3) | async-done | bytes 655392 | tf_op jit(solution)/shard_map/all_to_all | solution.py:115
  221.9 7.4 %all-to-all-start.1 = ((bf16[64,5,1024]{2,1,0:T(8,128)(2,1)}), bf16[64,5,1024]{2,1,0:T(8,128)(2,1)}, u32[]{:S(2)}, u32[]{:S(2)}) async-start(bf16[64,5,1024]{2,1,0:T(8,128)(2,1)} %reshape.163), calls=%async_computation.1 | async-start | bytes 2097152 | tf_op jit(solution)/shard_map/all_to_all | solution.py:112
  229.4 1.8 convert_element_type.67
  231.5 0.8 reshape_reshape.3
  232.2 2.0 constant_dynamic-slice_fusion
  234.9 4.1 %collective-permute-start = (bf16[320,128]{1,0:T(8,128)(2,1)}, bf16[320,128]{1,0:T(8,128)(2,1)}, u32[]{:S(2)}, u32[]{:S(2)}) collective-permute-start(bf16[320,128]{1,0:T(8,128)(2,1)} %bitcast.106), channel_id=1, source_target_pairs={{0,64},{64,0},{128,192},{192,128},{256,320},{320,256},{384,448},{4... | collective-permute-start | bytes 245768 | tf_op jit(solution)/shard_map/ppermute | solution.py:24
  239.0 0.8 all_to_all.30
  239.8 1.0 copy.37
  240.8 1.6 copy.57
  243.0 3.1 collective-permute-start.1
  246.2 2.3 collective-permute-start.2
  248.5 4.7 %collective-permute-start.3 = (bf16[320,128]{1,0:T(8,128)(2,1)S(1)}, bf16[320,128]{1,0:T(8,128)(2,1)S(1)}, u32[]{:S(2)}, u32[]{:S(2)}) collective-permute-start(bf16[320,128]{1,0:T(8,128)(2,1)S(1)} %bitcast.111), channel_id=1, source_target_pairs={{0,256},{64,320},{128,384},{192,448},{256,0},{320,64},{384,128},{4... | collective-permute-start | bytes 245768 | tf_op jit(solution)/shard_map/ppermute | solution.py:24
  253.2 2.5 collective-permute-start.4
  255.7 4.4 %collective-permute-start.5 = (bf16[320,128]{1,0:T(8,128)(2,1)}, bf16[320,128]{1,0:T(8,128)(2,1)S(1)}, u32[]{:S(2)}, u32[]{:S(2)}) collective-permute-start(bf16[320,128]{1,0:T(8,128)(2,1)} %bitcast.101), channel_id=1, source_target_pairs={{0,384},{64,448},{128,256},{192,320},{256,128},{320,192},{384,0},{... | collective-permute-start | bytes 245768 | tf_op jit(solution)/shard_map/ppermute | solution.py:24
  260.1 0.9 bitcast_dynamic-update-slice_fusion.7
  261.0 2.3 collective-permute-start.6
  263.4 17.5 %all-to-all-done.1 = bf16[64,5,1024]{2,1,0:T(8,128)(2,1)} async-done(((bf16[64,5,1024]{2,1,0:T(8,128)(2,1)}), bf16[64,5,1024]{2,1,0:T(8,128)(2,1)}, u32[]{:S(2)}, u32[]{:S(2)}) %all-to-all-start.1) | async-done | bytes 655392 | tf_op jit(solution)/shard_map/all_to_all | solution.py:112
  280.9 8.3 %all-to-all-start.4 = ((bf16[320,8,128]{2,0,1:T(8,128)(2,1)}), bf16[320,8,128]{2,0,1:T(8,128)(2,1)S(1)}, u32[]{:S(2)}, u32[]{:S(2)}) async-start(bf16[320,8,128]{2,0,1:T(8,128)(2,1)} %copy.37), calls=%async_computation.4 | async-start | bytes 1310720 | tf_op jit(solution)/shard_map/all_to_all | solution.py:130
  289.2 1.5 gather_fusion.2
  291.0 1.2 gather_fusion.1
  292.4 1.4 reshape.164
  293.8 1.2 gather_fusion
  295.8 3.6 %multiply_reduce_fusion = (f32[128,2]{1,0:T(8,128)S(1)}, bf16[128,1024]{1,0:T(8,128)(2,1)}) fusion(f32[128,2,1024]{2,1,0:T(2,128)S(1)} %reshape.171, f32[128,1024]{1,0:T(8,128)} %convert_element_type.67, f32[128,2]{1,0:T(8,128)S(1)} %copy-done.9), kind=kLoop, calls=%fused_computation.23 | loop fusion | flops 917248 | bytes 1837056 | tf_op jit(solution)/shard_map/reduce_sum | solution.py:128
  300.1 2.1 reduce_sum.60
  302.1 3.6 %convolution_bitcast_fusion.2 = f32[1,128,768]{2,1,0:T(8,128)} fusion(bf16[2560,128]{1,0:T(8,128)(2,1)S(1)} %bitcast.107, bf16[2560,768]{1,0:T(8,128)(2,1)} %all-gather.13.cloned.1.call-done), kind=kOutput, calls=%fused_computation.22 | convolution fusion | flops 503316480 | bytes 4980736 | tf_op jit(solution)/shard_map/dot_general | solution.py:50
  305.7 3.7 %convolution_bitcast_fusion.1 = f32[1,128,768]{2,1,0:T(8,128)} fusion(bf16[2560,128]{1,0:T(8,128)(2,1)S(1)} %bitcast.108, bf16[2560,768]{1,0:T(8,128)(2,1)} %all-gather.15.cloned.1.call-done), kind=kOutput, calls=%fused_computation.21 | convolution fusion | flops 503316480 | bytes 4980736 | tf_op jit(solution)/shard_map/dot_general | solution.py:50
  309.4 3.6 %convolution_bitcast_fusion = f32[1,128,768]{2,1,0:T(8,128)} fusion(bf16[2560,128]{1,0:T(8,128)(2,1)S(1)} %bitcast.109, bf16[2560,768]{1,0:T(8,128)(2,1)} %all-gather.17.cloned.1.call-done), kind=kOutput, calls=%fused_computation.20 | convolution fusion | flops 503316480 | bytes 4980736 | tf_op jit(solution)/shard_map/dot_general | solution.py:50
  (86 shorter events, 8.5 us)
Async XLA Ops:
  7.2 3.1 copy-start
  7.2 138.6 %all-gather.9.cloned.1.call-start = ((), (), s32[]{:S(2)}) async-start(), calls=%async_computation.6 | async-start | bytes 1769472 | tf_op jit(solution)/shard_map/all_gather | solution.py:84
  10.6 21.4 %copy-start.10 = (f32[128,2]{0,1:T(2,128)S(1)}, f32[128,2]{0,1:T(2,128)}, u32[]{:S(2)}) copy-start(f32[128,2]{0,1:T(2,128)} %param.9) | copy-start | bytes 3076
  11.8 20.9 %copy-start.7 = (bf16[128,1024]{1,0:T(8,128)(2,1)S(1)}, bf16[128,1024]{1,0:T(8,128)(2,1)}, u32[]{:S(2)}) copy-start(bf16[128,1024]{1,0:T(8,128)(2,1)} %param.8) | copy-start | bytes 786436
  11.8 71.7 %all-to-all-start = ((bf16[64,5,1024]{2,1,0:T(8,128)(2,1)}), bf16[64,5,1024]{2,1,0:T(8,128)(2,1)S(1)}, u32[]{:S(2)}, u32[]{:S(2)}) async-start(bf16[64,5,1024]{2,1,0:T(8,128)(2,1)} %reshape.161), calls=%async_computation | async-start | bytes 2097152 | tf_op jit(solution)/shard_map/all_to_all | solution.py:95
  31.2 117.6 %all-gather.11.cloned.1.call-start = ((), (), s32[]{:S(2)}) async-start(), calls=%async_computation.7 | async-start | bytes 1769472 | tf_op jit(solution)/shard_map/all_gather | solution.py:85
  32.1 0.6 copy-start.8
  83.5 61.2 %all-to-all-start.2 = ((bf16[64,5,1024]{2,1,0:T(8,128)(2,1)}), bf16[64,5,1024]{2,1,0:T(8,128)(2,1)S(1)}, u32[]{:S(2)}, u32[]{:S(2)}) async-start(bf16[64,5,1024]{2,1,0:T(8,128)(2,1)} %reshape.165), calls=%async_computation.2 | async-start | bytes 2097152 | tf_op jit(solution)/shard_map/all_to_all | solution.py:98
  91.9 60.3 %all-gather.7.cloned.1.call-start = ((), (), s32[]{:S(2)}) async-start(), calls=%async_computation.5 | async-start | bytes 1769472 | tf_op jit(solution)/shard_map/all_gather | solution.py:83
  92.6 209.6 %all-gather.13.cloned.1.call-start = ((), (), s32[]{:S(2)}) async-start(), calls=%async_computation.8 | async-start | bytes 4423680 | tf_op jit(solution)/shard_map/all_gather | solution.py:133
  156.2 1.2 copy-start.4
  156.2 149.5 %all-gather.15.cloned.1.call-start = ((), (), s32[]{:S(2)}) async-start(), calls=%async_computation.9 | async-start | bytes 4423680 | tf_op jit(solution)/shard_map/all_gather | solution.py:134
  156.8 152.6 %all-gather.17.cloned.1.call-start = ((), (), s32[]{:S(2)}) async-start(), calls=%async_computation.10 | async-start | bytes 4423680 | tf_op jit(solution)/shard_map/all_gather | solution.py:135
  157.4 2.3 copy-start.5
  157.4 2.3 copy-start.6
  161.6 60.3 %all-to-all-start.3 = ((bf16[64,5,1024]{2,1,0:T(8,128)(2,1)}), bf16[64,5,1024]{2,1,0:T(8,128)(2,1)S(1)}, u32[]{:S(2)}, u32[]{:S(2)}) async-start(bf16[64,5,1024]{2,1,0:T(8,128)(2,1)} %reshape.167), calls=%async_computation.3 | async-start | bytes 2097152 | tf_op jit(solution)/shard_map/all_to_all | solution.py:115
  221.9 9.5 %copy-start.1 = (bf16[64,5,1024]{2,1,0:T(8,128)(2,1)}, bf16[64,5,1024]{2,1,0:T(8,128)(2,1)S(1)}, u32[]{:S(2)}) copy-start(bf16[64,5,1024]{2,1,0:T(8,128)(2,1)S(1)} %all-to-all-done.3) | copy-start | bytes 1966084
  221.9 59.0 %all-to-all-start.1 = ((bf16[64,5,1024]{2,1,0:T(8,128)(2,1)}), bf16[64,5,1024]{2,1,0:T(8,128)(2,1)}, u32[]{:S(2)}, u32[]{:S(2)}) async-start(bf16[64,5,1024]{2,1,0:T(8,128)(2,1)} %reshape.163), calls=%async_computation.1 | async-start | bytes 2097152 | tf_op jit(solution)/shard_map/all_to_all | solution.py:112
  234.9 20.8 %collective-permute-start = (bf16[320,128]{1,0:T(8,128)(2,1)}, bf16[320,128]{1,0:T(8,128)(2,1)}, u32[]{:S(2)}, u32[]{:S(2)}) collective-permute-start(bf16[320,128]{1,0:T(8,128)(2,1)} %bitcast.106), channel_id=1, source_target_pairs={{0,64},{64,0},{128,192},{192,128},{256,320},{320,256},{384,448},{4... | collective-permute-start | bytes 245768 | tf_op jit(solution)/shard_map/ppermute | solution.py:24
  243.0 18.0 %collective-permute-start.1 = (bf16[320,128]{1,0:T(8,128)(2,1)S(1)}, bf16[320,128]{1,0:T(8,128)(2,1)S(1)}, u32[]{:S(2)}, u32[]{:S(2)}) collective-permute-start(bf16[320,128]{1,0:T(8,128)(2,1)S(1)} %bitcast.113), channel_id=1, source_target_pairs={{0,128},{64,192},{128,0},{192,64},{256,384},{320,448},{384,256},{4... | collective-permute-start | bytes 245768 | tf_op jit(solution)/shard_map/ppermute | solution.py:24
  246.2 17.2 %collective-permute-start.2 = (bf16[320,128]{1,0:T(8,128)(2,1)S(1)}, bf16[320,128]{1,0:T(8,128)(2,1)S(1)}, u32[]{:S(2)}, u32[]{:S(2)}) collective-permute-start(bf16[320,128]{1,0:T(8,128)(2,1)S(1)} %bitcast.112), channel_id=1, source_target_pairs={{0,192},{64,128},{128,64},{192,0},{256,448},{320,384},{384,320},{4... | collective-permute-start | bytes 245768 | tf_op jit(solution)/shard_map/ppermute | solution.py:24
  248.5 14.8 %collective-permute-start.3 = (bf16[320,128]{1,0:T(8,128)(2,1)S(1)}, bf16[320,128]{1,0:T(8,128)(2,1)S(1)}, u32[]{:S(2)}, u32[]{:S(2)}) collective-permute-start(bf16[320,128]{1,0:T(8,128)(2,1)S(1)} %bitcast.111), channel_id=1, source_target_pairs={{0,256},{64,320},{128,384},{192,448},{256,0},{320,64},{384,128},{4... | collective-permute-start | bytes 245768 | tf_op jit(solution)/shard_map/ppermute | solution.py:24
  253.2 10.2 %collective-permute-start.4 = (bf16[320,128]{1,0:T(8,128)(2,1)S(1)}, bf16[320,128]{1,0:T(8,128)(2,1)S(1)}, u32[]{:S(2)}, u32[]{:S(2)}) collective-permute-start(bf16[320,128]{1,0:T(8,128)(2,1)S(1)} %bitcast.110), channel_id=1, source_target_pairs={{0,320},{64,256},{128,448},{192,384},{256,64},{320,0},{384,192},{4... | collective-permute-start | bytes 245768 | tf_op jit(solution)/shard_map/ppermute | solution.py:24
  255.7 33.5 %collective-permute-start.5 = (bf16[320,128]{1,0:T(8,128)(2,1)}, bf16[320,128]{1,0:T(8,128)(2,1)S(1)}, u32[]{:S(2)}, u32[]{:S(2)}) collective-permute-start(bf16[320,128]{1,0:T(8,128)(2,1)} %bitcast.101), channel_id=1, source_target_pairs={{0,384},{64,448},{128,256},{192,320},{256,128},{320,192},{384,0},{... | collective-permute-start | bytes 245768 | tf_op jit(solution)/shard_map/ppermute | solution.py:24
  261.0 28.2 %collective-permute-start.6 = (bf16[320,128]{1,0:T(8,128)(2,1)}, bf16[320,128]{1,0:T(8,128)(2,1)S(1)}, u32[]{:S(2)}, u32[]{:S(2)}) collective-permute-start(bf16[320,128]{1,0:T(8,128)(2,1)} %bitcast.100), channel_id=1, source_target_pairs={{0,448},{64,384},{128,320},{192,256},{256,192},{320,128},{384,64},... | collective-permute-start | bytes 245768 | tf_op jit(solution)/shard_map/ppermute | solution.py:24
  263.4 27.3 %copy-start.2 = (bf16[64,5,1024]{2,1,0:T(8,128)(2,1)S(1)}, bf16[64,5,1024]{2,1,0:T(8,128)(2,1)}, u32[]{:S(2)}) copy-start(bf16[64,5,1024]{2,1,0:T(8,128)(2,1)} %copy-done.1) | copy-start | bytes 1966084
  280.9 21.2 %all-to-all-start.4 = ((bf16[320,8,128]{2,0,1:T(8,128)(2,1)}), bf16[320,8,128]{2,0,1:T(8,128)(2,1)S(1)}, u32[]{:S(2)}, u32[]{:S(2)}) async-start(bf16[320,8,128]{2,0,1:T(8,128)(2,1)} %copy.37), calls=%async_computation.4 | async-start | bytes 1310720 | tf_op jit(solution)/shard_map/all_to_all | solution.py:130
  295.0 0.8 copy-start.9
  305.7 3.7 %copy-start.3 = (bf16[8,320,128]{2,1,0:T(8,128)(2,1)S(1)}, bf16[8,320,128]{2,1,0:T(8,128)(2,1)}, u32[]{:S(2)}) copy-start(bf16[8,320,128]{2,1,0:T(8,128)(2,1)} %gather_fusion.2) | copy-start | bytes 1966084
Sparse Core Ops, SparseCore 0:
  10.1 37.8 all-gather.8
  50.2 32.1 all-gather.10
  94.8 34.0 all-gather.6
  156.3 33.3 all-gather.12
  191.7 38.6 all-gather.14
  232.4 45.7 all-gather.16
